TPU v7x, 1024 devices: a whole 4x4x32 slice. The times are simulated.
1024 devices in a mesh: dp: 4 (over x), expert: 8 (over y, core), tensor: 32 (over z).
Axes of the slice: x: 4, y: 4, z: 32, core: 2. Of those that a mesh axis runs over, the one named last changes fastest.
Arguments:
- tokens: bfloat16 [2048, 4096], P(('dp', 'expert'), 'tensor'), may hold values from -6 to 6
- cotangent: bfloat16 [2048, 4096], P(('dp', 'expert'), 'tensor'), may hold values from -6 to 6
- routes: int32 [2048, 2], P(('dp', 'expert')), may hold values from 0 to 7, all different within a row; in each aligned block of 64 rows (0 to 63, 64 to 127, ...) at most 24 rows name the same one
- gates: float32 [2048, 2], P(('dp', 'expert')), may hold values from 0.2 to 1
- w_gate: bfloat16 [8, 4096, 12288], P('expert', None, 'tensor'), may hold values from -0.1875 to 0.1875
- w_up: bfloat16 [8, 4096, 12288], P('expert', None, 'tensor'), may hold values from -0.1875 to 0.1875
- w_down: bfloat16 [8, 12288, 4096], P('expert', 'tensor'), may hold values from -0.109375 to 0.109375
Outputs:
- mixed: bfloat16 [2048, 4096], P(('dp', 'expert'), 'tensor')
- grad_input: bfloat16 [2048, 4096], P(('dp', 'expert'), 'tensor')
Inputs may be any that keep to these rules, and one draw needn't show every extreme that they name: `routes`: each token names 2 different experts. Within each aligned block of 64 tokens no expert is named by more than 24 tokens, and in some blocks one expert is named by exactly 24.
All inputs are finite; a program needn't handle non-finite values.
Results may differ from a plain program's by a relative error of at most 0.03.
Values may be sent and summed in bfloat16 or wider, within the bound.
A program may use at most 64 MiB of HBM per device.

v0:
```python
import jax
import jax.numpy as jnp
from jax import lax
from jax.sharding import PartitionSpec as P


def hidden_grads(gate, up, grad_hidden):
    sigmoid_gate = jax.nn.sigmoid(gate)
    active = gate * sigmoid_gate
    grad_gate = (grad_hidden * up * sigmoid_gate * (1.0 + gate * (1.0 - sigmoid_gate))).astype(
        jnp.bfloat16
    )
    grad_up = (grad_hidden * active).astype(jnp.bfloat16)
    return (grad_gate, grad_up)


def hidden_acts(gate, up):
    return (gate * jax.nn.sigmoid(gate) * up).astype(jnp.bfloat16)


def input_terms(grad_gate, grad_up, gate_local, up_local):
    terms = lax.dot_general(
        grad_gate, gate_local, (((1,), (1,)), ((), ())), preferred_element_type=jnp.float32
    )
    return terms + lax.dot_general(
        grad_up, up_local, (((1,), (1,)), ((), ())), preferred_element_type=jnp.float32
    )


def shards(tokens, cotangent, routes, gates, w_gate, w_up, w_down):
    groups = lax.axis_size("expert")
    tok_rows = tokens.shape[0]
    columns = tokens.shape[1]
    chosen = routes.shape[1]
    capacity = tok_rows * chosen * 3 // (2 * groups)
    slot_rows = groups * capacity
    flat_routes = routes.reshape(-1)
    onehot = flat_routes[:, None] == jnp.arange(groups, dtype=jnp.int32)[None, :]
    running = jnp.cumsum(onehot.astype(jnp.int32), axis=0) - 1
    slot = jnp.sum(jnp.where(onehot, running, 0), axis=1)
    target = flat_routes * capacity + slot
    placing = (jnp.arange(slot_rows, dtype=jnp.int32)[:, None] == target[None, :]).astype(
        jnp.bfloat16
    )
    token_rows = jnp.repeat(tokens, chosen, axis=0)
    weighted = (
        jnp.repeat(cotangent.astype(jnp.float32), chosen, axis=0) * gates.reshape(-1)[:, None]
    ).astype(jnp.bfloat16)
    send_tokens = (
        jnp.dot(placing, token_rows, preferred_element_type=jnp.float32)
        .astype(jnp.bfloat16)
        .reshape(groups, capacity, columns)
    )
    send_grads = (
        jnp.dot(placing, weighted, preferred_element_type=jnp.float32)
        .astype(jnp.bfloat16)
        .reshape(groups, capacity, columns)
    )
    recv_tokens, recv_grads = (
        lax.all_to_all(send_tokens, "expert", split_axis=0, concat_axis=0, tiled=True),
        lax.all_to_all(send_grads, "expert", split_axis=0, concat_axis=0, tiled=True),
    )
    recv_tokens = recv_tokens.reshape(slot_rows, columns)
    recv_grads = recv_grads.reshape(slot_rows, columns)
    gate_local = w_gate[0]
    up_local = w_up[0]
    down_local = w_down[0]
    piece = lax.all_gather(recv_tokens, "tensor", axis=1, tiled=True)
    gate_sum = jnp.dot(piece, gate_local, preferred_element_type=jnp.float32)
    up_sum = jnp.dot(piece, up_local, preferred_element_type=jnp.float32)
    grad_hidden = lax.dot_general(
        lax.all_gather(recv_grads, "tensor", axis=1, tiled=True),
        down_local,
        (((1,), (1,)), ((), ())),
        preferred_element_type=jnp.float32,
    )
    hidden = hidden_acts(gate_sum, up_sum)
    out_terms = jnp.dot(hidden, down_local, preferred_element_type=jnp.float32)
    grad_gate, grad_up = hidden_grads(gate_sum, up_sum, grad_hidden)
    grad_terms = input_terms(grad_gate, grad_up, gate_local, up_local)
    out_part, grad_part = (
        lax.psum_scatter(
            out_terms.astype(jnp.bfloat16), "tensor", scatter_dimension=1, tiled=True
        ).astype(jnp.float32),
        lax.psum_scatter(
            grad_terms.astype(jnp.bfloat16), "tensor", scatter_dimension=1, tiled=True
        ).astype(jnp.float32),
    )
    back_out = out_part.astype(jnp.bfloat16).reshape(groups, capacity, columns)
    back_grad = grad_part.astype(jnp.bfloat16).reshape(groups, capacity, columns)
    home_out, home_grad = (
        lax.all_to_all(back_out, "expert", split_axis=0, concat_axis=0, tiled=True),
        lax.all_to_all(back_grad, "expert", split_axis=0, concat_axis=0, tiled=True),
    )
    picked_out = lax.dot_general(
        placing,
        home_out.reshape(slot_rows, columns),
        (((0,), (0,)), ((), ())),
        preferred_element_type=jnp.float32,
    )
    picked_grad = lax.dot_general(
        placing,
        home_grad.reshape(slot_rows, columns),
        (((0,), (0,)), ((), ())),
        preferred_element_type=jnp.float32,
    )
    mixed = jnp.sum(
        picked_out.reshape(tok_rows, chosen, columns) * gates[:, :, None], axis=1
    ).astype(jnp.bfloat16)
    grad_input = jnp.sum(picked_grad.reshape(tok_rows, chosen, columns), axis=1).astype(
        jnp.bfloat16
    )
    return (mixed, grad_input)


def solution(mesh):
    return jax.shard_map(
        shards,
        mesh=mesh,
        in_specs=(
            P(("dp", "expert"), "tensor"),
            P(("dp", "expert"), "tensor"),
            P(("dp", "expert"), None),
            P(("dp", "expert"), None),
            P("expert", None, "tensor"),
            P("expert", None, "tensor"),
            P("expert", "tensor", None),
        ),
        out_specs=(P(("dp", "expert"), "tensor"), P(("dp", "expert"), "tensor")),
        check_vma=False,
    )
```

profile of v0, /device:TPU:1, one launch (start us, length us, event | category | flops | bytes accessed | tf_op | source)
XLA Modules:
  0.0 583.9 jit_solution(16556813572680678042)
XLA Ops:
  7.2 0.9 copy.15
  8.4 0.2 reduce_window_sum.11
  8.6 0.2 select_reduce_fusion
  8.7 0.7 broadcast_in_dim.15
  9.5 0.1 convolution_convert_fusion.2
  9.6 22.0 %all_to_all.20 = bf16[8,24,128]{2,1,0:T(8,128)(2,1)} all-to-all(bf16[8,24,128]{2,1,0:T(8,128)(2,1)S(1)} %bitcast.45), channel_id=1, replica_groups=mesh['dp'=4,'expert'=8,'tensor'=32] {'expert'}, dimensions={0} | all-to-all | bytes 98304 | tf_op jit(solution)/shard_map/all_to_all | solution.py:60
  31.7 0.8 copy.17
  32.6 0.7 broadcast_in_dim.16
  33.3 0.2 convolution_convert_fusion.1
  33.6 8.6 %all_to_all.21 = bf16[8,24,128]{2,1,0:T(8,128)(2,1)} all-to-all(bf16[8,24,128]{2,1,0:T(8,128)(2,1)S(1)} %bitcast.42), channel_id=1, replica_groups=mesh['dp'=4,'expert'=8,'tensor'=32] {'expert'}, dimensions={0} | all-to-all | bytes 98304 | tf_op jit(solution)/shard_map/all_to_all | solution.py:61
  42.2 100.7 %all-gather.3.cloned.1.call-done = bf16[192,4096]{1,0:T(8,128)(2,1)} async-done(((bf16[192,128]{1,0:T(8,128)(2,1)}), bf16[192,4096]{1,0:T(8,128)(2,1)}) %all-gather.3.cloned.1.call-update) | async-done | bytes 1572880 | tf_op jit(solution)/shard_map/all_gather | solution.py:68
  142.9 3.5 fusion.9
  146.4 0.3 copy-done.4
  146.7 1.0 fusion.5
  147.7 0.7 copy-done.5
  148.4 2.2 convolution_convert_fusion
  150.6 3.8 copy.19
  154.5 121.1 %all-gather.5.cloned.1.call-done = bf16[192,4096]{1,0:T(8,128)(2,1)} async-done(((bf16[192,128]{1,0:T(8,128)(2,1)}), bf16[192,4096]{1,0:T(8,128)(2,1)}) %all-gather.5.cloned.1.call-update) | async-done | bytes 1572880 | tf_op jit(solution)/shard_map/all_gather | solution.py:72
  275.6 2.7 fusion.1
  278.4 1.3 fusion.7
  279.6 0.6 copy-done.3
  280.3 2.4 fusion
  282.7 3.8 copy.21
  286.6 120.8 %reduce-scatter.7.cloned.1.call-done = bf16[128,192]{1,0:T(8,128)(2,1)} async-done(((bf16[4096,192]{1,0:T(8,128)(2,1)}), bf16[128,192]{1,0:T(8,128)(2,1)}) %reduce-scatter.7.cloned.1.call-update) | async-done | bytes 49168
  407.4 1.5 copy.20
  408.9 26.5 %all-to-all-start.1 = ((bf16[8,24,128]{2,1,0:T(8,128)(2,1)}), bf16[8,24,128]{2,1,0:T(8,128)(2,1)S(1)}, u32[]{:S(2)}, u32[]{:S(2)}) async-start(bf16[8,24,128]{2,1,0:T(8,128)(2,1)} %bitcast.6), calls=%async_computation.1 | async-start | bytes 98304 | tf_op jit(solution)/shard_map/all_to_all | solution.py:92
  435.6 109.1 %reduce-scatter.9.cloned.1.call-done = bf16[128,192]{1,0:T(8,128)(2,1)} async-done(((bf16[4096,192]{1,0:T(8,128)(2,1)}), bf16[128,192]{1,0:T(8,128)(2,1)}) %reduce-scatter.9.cloned.1.call-update) | async-done | bytes 49168
  544.7 1.6 copy.22
  546.2 25.6 %all-to-all-start.3 = ((bf16[8,24,128]{2,1,0:T(8,128)(2,1)}), bf16[8,24,128]{2,1,0:T(8,128)(2,1)S(1)}, u32[]{:S(2)}, u32[]{:S(2)}) async-start(bf16[8,24,128]{2,1,0:T(8,128)(2,1)} %bitcast.12), calls=%async_computation.3 | async-start | bytes 98304 | tf_op jit(solution)/shard_map/all_to_all | solution.py:93
  571.9 0.8 fusion.11
  572.6 4.0 all-to-all-done.3
  576.6 0.8 convolution_reduce_fusion
  (28 shorter events, 0.8 us)
Async XLA Ops:
  7.2 141.3 %copy-start = (bf16[1,384,4096]{2,1,0:T(8,128)(2,1)S(1)}, bf16[1,384,4096]{2,1,0:T(8,128)(2,1)}, u32[]{:S(2)}) copy-start(bf16[1,384,4096]{2,1,0:T(8,128)(2,1)} %param.13) | copy-start | bytes 9437188
  7.2 135.8 %all-gather.3.cloned.1.call-start = ((), (), s32[]{:S(2)}) async-start(), calls=%async_computation.6 | async-start | bytes 1622016 | tf_op jit(solution)/shard_map/all_gather | solution.py:68
  31.6 244.0 %all-gather.5.cloned.1.call-start = ((), (), s32[]{:S(2)}) async-start(), calls=%async_computation.7 | async-start | bytes 1622016 | tf_op jit(solution)/shard_map/all_gather | solution.py:72
  42.2 365.2 %reduce-scatter.7.cloned.1.call-start = ((), (), s32[]{:S(2)}) async-start(), calls=%async_computation.8 | async-start | bytes 2162688
  142.9 3.5 copy-start.2
  142.9 3.8 copy-start.4
  147.7 0.7 copy-start.5
  154.5 390.2 %reduce-scatter.9.cloned.1.call-start = ((), (), s32[]{:S(2)}) async-start(), calls=%async_computation.9 | async-start | bytes 2162688
  275.6 2.7 copy-start.1
  275.6 2.8 copy-start.6
  278.4 1.9 copy-start.3
  282.7 289.2 %copy-start.7 = (f32[64,2]{0,1:T(2,128)S(1)}, f32[64,2]{0,1:T(2,128)}, u32[]{:S(2)}) copy-start(f32[64,2]{0,1:T(2,128)} %param.10) | copy-start | bytes 1540
  408.9 137.3 %all-to-all-start.1 = ((bf16[8,24,128]{2,1,0:T(8,128)(2,1)}), bf16[8,24,128]{2,1,0:T(8,128)(2,1)S(1)}, u32[]{:S(2)}, u32[]{:S(2)}) async-start(bf16[8,24,128]{2,1,0:T(8,128)(2,1)} %bitcast.6), calls=%async_computation.1 | async-start | bytes 98304 | tf_op jit(solution)/shard_map/all_to_all | solution.py:92
  546.2 30.4 %all-to-all-start.3 = ((bf16[8,24,128]{2,1,0:T(8,128)(2,1)}), bf16[8,24,128]{2,1,0:T(8,128)(2,1)S(1)}, u32[]{:S(2)}, u32[]{:S(2)}) async-start(bf16[8,24,128]{2,1,0:T(8,128)(2,1)} %bitcast.12), calls=%async_computation.3 | async-start | bytes 98304 | tf_op jit(solution)/shard_map/all_to_all | solution.py:93
Sparse Core Ops, SparseCore 0:
  31.8 111.1 all-gather.2
  145.5 130.0 all-gather.4
  279.0 128.3 reduce-scatter.6
  411.0 133.6 reduce-scatter.8
where the time goes:
time: 585 us; the launch traced here: 584 us
  waiting for transfers between devices  456 us (78%)
  starting transfers between devices  52.3 us (9%)
  blocking collectives  30.6 us (5%)
  local copies, waits for them, and re-layouts  15.9 us (3%)
  matrix products  14.9 us (3%)
  between operations  13.9 us (2%)
    unnamed x6, waiting for transfers between devices  230 us
    all_gather x1, waiting for transfers between devices, shards(): lax.all_gather(recv_grads, 'tensor', axis=1, tiled=True)  121 us
    all_gather x1, waiting for transfers between devices, shards(): piece = lax.all_gather(recv_tokens, 'tensor', axis=1, tiled=True)  101 us
    all_to_all x1, starting transfers between devices, shards(): lax.all_to_all(back_out, 'expert', split_axis=0, concat_axis=0, tiled=True)  26.5 us
    all_to_all x1, starting transfers between devices, shards(): lax.all_to_all(back_grad, 'expert', split_axis=0, concat_axis=0, tiled=True)  25.6 us
    all_to_all x1, blocking collectives, shards(): lax.all_to_all(send_tokens, 'expert', split_axis=0, concat_axis=0, tiled=...  22 us
    unnamed x22, local copies, waits for them, and re-layouts  14.1 us
  transfers between devices with their start and end apart: 6, of which 5 were waited for; matrix products, arithmetic and copies ran while one was open for 5% of the time, Pallas kernels for 0%

commit v1 on v0

v1 whole, which is shorter than its diff:
```python
import functools

import jax
import jax.numpy as jnp
from jax import lax
from jax.experimental import pallas as pl
from jax.experimental.pallas import tpu as pltpu
from jax.sharding import PartitionSpec as P

MESH = pl.DeviceIdType.MESH
F32 = jnp.float32
BF16 = jnp.bfloat16
NT = (((1,), (1,)), ((), ()))


def kernel(
    cap,
    nz,
    tok_ref,
    cot_ref,
    routes_ref,
    gates_ref,
    wg_hbm,
    wu_hbm,
    wd_hbm,
    mixed_ref,
    grad_ref,
    wg,
    wu,
    wd,
    raw,
    stage,
    even,
    odd,
    acc,
    hid,
    gg,
    gu,
    qt_ref,
    gs_ref,
    pick_ref,
    odd_out,
    odd_in,
    back,
    home,
    chain_out,
    chain_in,
    w_sem,
    raw_s,
    raw_r,
    y_s,
    y_r,
    odd_s,
    odd_r,
    po_s,
    po_r,
    b_s,
    b_r,
    c_s,
    c_r,
):
    dp, me, z = lax.axis_index("dp"), lax.axis_index("expert"), lax.axis_index("tensor")
    ne = lax.axis_size("expert")
    toks, cols = tok_ref.shape
    hidden = wd.shape[0]
    pair = 2 * cap
    rows = ne * pair
    last = nz // 4

    def at_z(offset):
        return (dp, me, lax.rem(z + offset + nz, nz))

    def peer(i):
        return (dp, lax.rem(me + i, ne), z)

    def remote(src, dst, send, recv, device):
        return pltpu.make_async_remote_copy(
            src_ref=src, dst_ref=dst, send_sem=send, recv_sem=recv, device_id=device, device_id_type=MESH
        )

    def feat(offset):
        return pl.ds(pl.multiple_of(lax.rem(z + offset + nz, nz) * cols, cols), cols)

    loads = [
        pltpu.make_async_copy(src, dst, w_sem.at[i])
        for i, (src, dst) in enumerate(((wg_hbm.at[0], wg), (wu_hbm.at[0], wu), (wd_hbm.at[0], wd)))
    ]
    barrier = pltpu.get_barrier_semaphore()
    greeted = [at_z(1), at_z(-1), at_z(2), at_z(-2)] + [peer(i) for i in range(1, ne)]
    for device in greeted:
        pl.semaphore_signal(barrier, inc=1, device_id=device, device_id_type=MESH)
    for load in loads:
        load.start()

    raw[0, 0:toks, :] = tok_ref[...]
    raw[0, toks : 2 * toks, :] = cot_ref[...]
    lane = lax.broadcasted_iota(jnp.int32, (toks, 128), 1)
    chosen = [(routes_ref[:, k : k + 1] == lane).astype(F32) for k in range(2)]
    before = (
        lax.broadcasted_iota(jnp.int32, (toks, toks), 1) < lax.broadcasted_iota(jnp.int32, (toks, toks), 0)
    ).astype(BF16)
    counts = jnp.dot(before, (chosen[0] + chosen[1]).astype(BF16), preferred_element_type=F32)
    target = [
        jnp.sum(chosen[k] * (counts + (lane * pair).astype(F32)), axis=1, keepdims=True) for k in range(2)
    ]
    wide = lax.broadcasted_iota(jnp.int32, (toks, rows), 1).astype(F32)
    for k in range(2):
        pick_ref[k * toks : (k + 1) * toks, :] = (wide == target[k]).astype(BF16)
    pick_ref[2 * toks : 3 * toks, :] = (
        (wide == target[0] + cap).astype(F32) + (wide == target[1] + cap).astype(F32)
    ).astype(BF16)
    token = lax.broadcasted_iota(jnp.int32, (toks, 2 * toks), 0)
    column = lax.broadcasted_iota(jnp.int32, (toks, 2 * toks), 1)
    diagonal = (column == token) | (column == token + toks)
    down_rows = lax.broadcasted_iota(jnp.int32, (rows, 2 * toks), 0).astype(F32)
    lanes1 = lax.broadcasted_iota(jnp.int32, (1, 2 * toks), 1)
    second = jnp.where(lanes1 < toks, 0.0, float(cap))
    placing, scale = 0.0, 0.0
    for k in range(2):
        row_target = jnp.sum(jnp.where(diagonal, target[k], 0.0), axis=0, keepdims=True) + second
        row_gate = jnp.sum(jnp.where(diagonal, gates_ref[:, k : k + 1], 0.0), axis=0, keepdims=True)
        row_gate = jnp.where(lanes1 < toks, 1.0, row_gate)
        hit = down_rows == row_target
        placing = placing + hit.astype(F32)
        scale = scale + jnp.sum(jnp.where(hit, row_gate, 0.0), axis=1, keepdims=True)
    qt_ref[...] = placing.astype(BF16)
    gs_ref[...] = jnp.broadcast_to(scale, (rows, 128))

    pl.semaphore_wait(barrier, len(greeted))

    def raw_copy(k, d):
        src = raw.at[0] if isinstance(k, int) and k == 1 else raw.at[2 * k - 3 + d]
        i = 2 * k - 1 + d
        return remote(src, raw.at[i], raw_s.at[i], raw_r.at[i], at_z(2 - 4 * d))

    def raw_last(d):
        src = raw.at[2 * last - 3 + d, pl.ds(d * toks, toks)]
        dst = raw.at[2 * last - 1, pl.ds(d * toks, toks)]
        i = 2 * last - 1 + d
        return remote(src, dst, raw_s.at[i], raw_r.at[i], at_z(2 - 4 * d))

    def single(k):
        return isinstance(k, int) and k in (0, last)

    def first_slice(k):
        return 0 if isinstance(k, int) and k == 0 else 2 * k - 1

    def y_copy(k, i, out, into, send, recv):
        to = lax.rem(me + i, ne)
        if single(k):
            return remote(out.at[k, to, 0], into.at[first_slice(k), me], send.at[k, i], recv.at[k, i], peer(i))
        return remote(
            out.at[k, to], into.at[pl.ds(2 * k - 1, 2), me], send.at[k, i], recv.at[k, i], peer(i)
        )

    def slices(k):
        return 1 if single(k) else 2

    def exchange(k, out, into, send, recv):
        for i in range(1, ne):
            y_copy(k, i, out, into, send, recv).start()
        for d in range(slices(k)):
            into[first_slice(k) + d, me] = out[k, me, d]

    def dispatch(k):
        n = slices(k)
        block = raw[first_slice(k)]
        if n == 2:
            block = jnp.concatenate([block, raw[2 * k]], axis=1)
        placed = jnp.dot(qt_ref[...], block, preferred_element_type=F32)
        for d in range(n):
            one = (placed[:, d * cols : (d + 1) * cols] * gs_ref[...]).astype(BF16)
            stage[k, :, d] = one.reshape(ne, pair, cols)
        exchange(k, stage, even, y_s, y_r)

    def odd_copy(k, d):
        src = even.at[0] if isinstance(k, int) and k == 0 else even.at[2 * k - 1 + d]
        i = 2 * k + d
        return remote(src, odd.at[i], odd_s.at[i], odd_r.at[i], at_z(1 - 2 * d))

    def pass_on(k):
        for i in range(1, ne):
            y_copy(k, i, stage, even, y_s, y_r).wait_recv()
        if not (isinstance(k, int) and k == last):
            for d in range(2):
                odd_copy(k, d).start()

    def accumulate(parts, first=False):
        lhs = [buf[i].reshape(rows, cols) for buf, i, _ in parts]
        lhs = lhs[0] if len(lhs) == 1 else jnp.concatenate(lhs, axis=1)
        for n, w in enumerate((wg, wu, wd)):
            if n < 2:
                rhs = [w[feat(o), :] for _, _, o in parts]
                rhs = rhs[0] if len(rhs) == 1 else jnp.concatenate(rhs, axis=0)
                term = jnp.dot(lhs, rhs, preferred_element_type=F32)
            else:
                rhs = [w[:, feat(o)] for _, _, o in parts]
                rhs = rhs[0] if len(rhs) == 1 else jnp.concatenate(rhs, axis=1)
                term = lax.dot_general(lhs, rhs, NT, preferred_element_type=F32)
            span = slice(n * hidden, (n + 1) * hidden)
            if first:
                acc[:, span] = term
            else:
                acc[:, span] += term

    def even_parts(k):
        return [(even, 2 * k - 1, -2 * k), (even, 2 * k, 2 * k)]

    def odd_parts(k):
        return [(odd, 2 * k, -2 * k - 1), (odd, 2 * k + 1, 2 * k + 1)]

    def odd_arrived(k):
        for d in range(2):
            odd_copy(k, d).wait_recv()

    def y_sent(k, out, into, send, recv):
        for i in range(1, ne):
            y_copy(k, i, out, into, send, recv).wait_send()

    for d in range(2):
        raw_copy(1, d).start()
    dispatch(0)
    for d in range(2):
        raw_copy(1, d).wait_recv()
    for d in range(2):
        raw_copy(2, d).start()
    dispatch(1)
    pass_on(0)
    for load in loads:
        load.wait()
    accumulate([(even, 0, 0)], first=True)
    for d in range(2):
        raw_copy(1, d).wait_send()

    def gather_step(k, forward):
        for d in range(2):
            raw_copy(k, d).wait_recv()
        forward()
        dispatch(k)
        pass_on(k - 1)
        odd_arrived(k - 2)
        accumulate(even_parts(k - 1) + odd_parts(k - 2))
        for d in range(2):
            raw_copy(k, d).wait_send()
            odd_copy(k - 2, d).wait_send()
        y_sent(k - 2, stage, even, y_s, y_r)

    def forward_next(k):
        for d in range(2):
            raw_copy(k + 1, d).start()

    def forward_last():
        for d in range(2):
            raw_last(d).start()

    gather_step(2, lambda: forward_next(2))

    def gather_loop(k, carry):
        gather_step(k, lambda: forward_next(k))
        return carry

    lax.fori_loop(3, last - 1, gather_loop, 0)
    gather_step(last - 1, forward_last)
    for d in range(2):
        raw_last(d).wait_recv()
    dispatch(last)
    pass_on(last - 1)
    odd_arrived(last - 2)
    accumulate(even_parts(last - 1) + odd_parts(last - 2))
    pass_on(last)
    odd_arrived(last - 1)
    accumulate([(even, 2 * last - 1, 2 * last)] + odd_parts(last - 1))

    for j in range(ne // 2):
        top = 2 * pair * j
        mine = jnp.concatenate([acc[top : top + cap, :], acc[top + pair : top + pair + cap, :]], axis=0)
        gh = jnp.concatenate(
            [acc[top + cap : top + pair, 2 * hidden :], acc[top + pair + cap : top + 2 * pair, 2 * hidden :]],
            axis=0,
        )
        gate, up = mine[:, :hidden], mine[:, hidden : 2 * hidden]
        sigmoid = jax.nn.sigmoid(gate)
        active = gate * sigmoid
        span = slice(pair * j, pair * (j + 1))
        hid[span, :] = (active * up).astype(BF16)
        gg[span, :] = (gh * up * sigmoid * (1.0 + gate * (1.0 - sigmoid))).astype(BF16)
        gu[span, :] = (gh * active).astype(BF16)

    def partial(offsets):
        down = [wd[:, feat(o)] for o in offsets]
        gate = [wg[feat(o), :] for o in offsets]
        up = [wu[feat(o), :] for o in offsets]
        if len(offsets) > 1:
            down = jnp.concatenate(down, axis=1)
            gate, up = jnp.concatenate(gate, axis=0), jnp.concatenate(up, axis=0)
        else:
            down, gate, up = down[0], gate[0], up[0]
        out = jnp.dot(hid[...], down, preferred_element_type=F32)
        grad = lax.dot_general(gg[...], gate, NT, preferred_element_type=F32)
        grad = grad + lax.dot_general(gu[...], up, NT, preferred_element_type=F32)
        parts = []
        for j in range(ne):
            parts += [out[cap * j : cap * (j + 1)], grad[cap * j : cap * (j + 1)]]
        return jnp.concatenate(parts, axis=0)

    def po_copy(k, d):
        i = 2 * k + d
        return remote(odd_out.at[i], odd_in.at[i], po_s.at[i], po_r.at[i], at_z(2 * d - 1))

    def send_odd(k):
        both = partial([-2 * k - 1, 2 * k + 1]).astype(BF16)
        for d in range(2):
            odd_out[2 * k + d] = both[:, d * cols : (d + 1) * cols]
            po_copy(k, d).start()

    def send_even(k):
        if isinstance(k, int) and k == last:
            total = [partial([2 * k])]
        elif isinstance(k, int) and k == 0:
            total = partial([0])
            for d in range(2):
                po_copy(0, d).wait_recv()
                total = total + odd_in[d].astype(F32)
            total = [total]
        else:
            both = partial([-2 * k, 2 * k])
            total = []
            for d in range(2):
                po_copy(k, d).wait_recv()
                total.append(both[:, d * cols : (d + 1) * cols] + odd_in[2 * k + d].astype(F32))
        for d in range(slices(k)):
            back[k, :, d] = total[d].astype(BF16).reshape(ne, pair, cols)
        exchange(k, back, home, b_s, b_r)

    def combine(k):
        for i in range(1, ne):
            y_copy(k, i, back, home, b_s, b_r).wait_recv()
        block = home[first_slice(k)].reshape(rows, cols)
        if slices(k) == 2:
            block = jnp.concatenate([block, home[2 * k].reshape(rows, cols)], axis=1)
        picked = jnp.dot(pick_ref[...], block, preferred_element_type=F32)
        mixed = gates_ref[:, 0:1] * picked[:toks] + gates_ref[:, 1:2] * picked[toks : 2 * toks]
        return mixed, picked[2 * toks :]

    def chain_copy(k, d):
        i = 2 * k - 2 + d
        return remote(
            chain_out.at[2 * k - 1 + d], chain_in.at[i], c_s.at[i], c_r.at[i], at_z(4 * d - 2)
        )

    def chain_first(d):
        i = 2 * last - 2 + d
        part = pl.ds(d * toks, toks)
        return remote(
            chain_out.at[2 * last - 1, part], chain_in.at[i, part], c_s.at[i], c_r.at[i], at_z(4 * d - 2)
        )

    def chain_step(k, halves=False):
        mixed, grad = combine(k)
        for d in range(2):
            span = slice(d * cols, (d + 1) * cols)
            i = 2 * k + d
            if halves:
                chain_first(d).wait_recv()
            else:
                chain_copy(k + 1, d).wait_recv()
            m, g = mixed[:, span], grad[:, span]
            if not halves or d == 0:
                m = m + chain_in[i, 0:toks, :].astype(F32)
            if not halves or d == 1:
                g = g + chain_in[i, toks : 2 * toks, :].astype(F32)
            chain_out[2 * k - 1 + d, 0:toks, :] = m.astype(BF16)
            chain_out[2 * k - 1 + d, toks : 2 * toks, :] = g.astype(BF16)
            chain_copy(k, d).start()

    send_odd(last - 1)
    send_even(last)
    send_odd(last - 2)
    send_even(last - 1)
    for d in range(2):
        raw_last(d).wait_send()
        odd_copy(last - 2, d).wait_send()
        odd_copy(last - 1, d).wait_send()
    for k in (last - 2, last - 1, last):
        y_sent(k, stage, even, y_s, y_r)
    mixed, grad = combine(last)
    chain_out[2 * last - 1, 0:toks, :] = mixed.astype(BF16)
    chain_out[2 * last - 1, toks : 2 * toks, :] = grad.astype(BF16)
    for d in range(2):
        chain_first(d).start()

    send_odd(last - 3)
    send_even(last - 2)
    chain_step(last - 1, halves=True)

    def back_loop(n, carry):
        k = last - 3 - n
        send_odd(k - 1)
        send_even(k)
        chain_step(k + 1)
        for d in range(2):
            po_copy(k + 2, d).wait_send()
            chain_copy(k + 2, d).wait_send()
        y_sent(k + 2, back, home, b_s, b_r)
        return carry

    lax.fori_loop(0, last - 3, back_loop, 0)
    send_even(0)
    chain_step(1)
    mixed, grad = combine(0)
    for d in range(2):
        chain_copy(1, d).wait_recv()
        mixed = mixed + chain_in[d, 0:toks, :].astype(F32)
        grad = grad + chain_in[d, toks : 2 * toks, :].astype(F32)
    mixed_ref[...] = mixed.astype(BF16)
    grad_ref[...] = grad.astype(BF16)
    for d in range(2):
        chain_first(d).wait_send()
        for k in (2, 1):
            chain_copy(k, d).wait_send()
        for k in (2, 1, 0):
            po_copy(k, d).wait_send()
    for k in (last, 2, 1, 0):
        y_sent(k, back, home, b_s, b_r)


def shards(tokens, cotangent, routes, gates, w_gate, w_up, w_down):
    ne, nz = lax.axis_size("expert"), lax.axis_size("tensor")
    toks, cols = tokens.shape
    width, hidden = w_gate.shape[1:]
    cap = toks * routes.shape[1] * 3 // (2 * ne)
    pair = 2 * cap
    rows = ne * pair
    steps = nz // 4 + 1
    half = nz // 2
    vmem = pl.BlockSpec(memory_space=pltpu.VMEM)
    anywhere = pl.BlockSpec(memory_space=pl.ANY)
    dma = pltpu.SemaphoreType.DMA
    out = jax.ShapeDtypeStruct((toks, cols), BF16)
    slab = pltpu.VMEM((half, ne, pair, cols), BF16)
    flat = pltpu.VMEM((half, rows, cols), BF16)
    staged = pltpu.VMEM((steps, ne, 2, pair, cols), BF16)
    return pl.pallas_call(
        functools.partial(kernel, cap, nz),
        out_shape=(out, out),
        in_specs=[vmem] * 4 + [anywhere] * 3,
        out_specs=(vmem, vmem),
        scratch_shapes=[
            pltpu.VMEM((width, hidden), BF16),
            pltpu.VMEM((width, hidden), BF16),
            pltpu.VMEM((hidden, width), BF16),
            pltpu.VMEM((half, 2 * toks, cols), BF16),
            staged,
            slab,
            slab,
            pltpu.VMEM((rows, 3 * hidden), F32),
            pltpu.VMEM((rows // 2, hidden), BF16),
            pltpu.VMEM((rows // 2, hidden), BF16),
            pltpu.VMEM((rows // 2, hidden), BF16),
            pltpu.VMEM((rows, 2 * toks), BF16),
            pltpu.VMEM((rows, 128), F32),
            pltpu.VMEM((3 * toks, rows), BF16),
            flat,
            flat,
            staged,
            slab,
            pltpu.VMEM((half, 2 * toks, cols), BF16),
            pltpu.VMEM((half, 2 * toks, cols), BF16),
            dma((3,)),
            dma((half + 1,)),
            dma((half + 1,)),
            dma((steps, ne)),
            dma((steps, ne)),
            dma((half,)),
            dma((half,)),
            dma((half,)),
            dma((half,)),
            dma((steps, ne)),
            dma((steps, ne)),
            dma((half,)),
            dma((half,)),
        ],
        name="moe_layer",
        cost_estimate=pl.CostEstimate(
            flops=12 * rows * width * hidden, bytes_accessed=6 * width * hidden, transcendentals=rows * hidden
        ),
        compiler_params=pltpu.CompilerParams(
            collective_id=0, has_side_effects=True, vmem_limit_bytes=48 * 1024 * 1024
        ),
    )(tokens, cotangent, routes, gates, w_gate, w_up, w_down)


def solution(mesh):
    return jax.shard_map(
        shards,
        mesh=mesh,
        in_specs=(
            P(("dp", "expert"), "tensor"),
            P(("dp", "expert"), "tensor"),
            P(("dp", "expert"), None),
            P(("dp", "expert"), None),
            P("expert", None, "tensor"),
            P("expert", None, "tensor"),
            P("expert", "tensor", None),
        ),
        out_specs=(P(("dp", "expert"), "tensor"), P(("dp", "expert"), "tensor")),
        check_vma=False,
    )
```

time: 585 us -> 111 us (0.19)
  waiting for transfers between devices: 456 us -> 0 us
  Pallas kernels: 0 us -> 103 us
  starting transfers between devices: 52.3 us -> 0 us
  blocking collectives: 30.6 us -> 0 us
  matrix products: 14.9 us -> 0 us
  between operations: 13.9 us -> 0.64 us
  local copies, waits for them, and re-layouts: 15.9 us -> 6.07 us
    unnamed x6 -> x0, waiting for transfers between devices: 230 us -> none
    all_gather x2 -> x0, waiting for transfers between devices: 222 us -> none  [the longest x1 121 us: shards(): lax.all_gather(recv_grads, 'tensor', axis=1, tiled=True)]
    pallas_call x0 -> x1, Pallas kernels: none -> 103 us  [shards(): pl.pallas_call(functools.partial(kernel, cap, nz), out_shape=(out, out),...]
    all_to_all x2 -> x0, starting transfers between devices: 52.1 us -> none  [the longest x1 26.5 us: shards(): lax.all_to_all(back_out, 'expert', split_axis=0, concat_axis=0, tiled=True)]
    all_to_all x2 -> x0, blocking collectives: 30.6 us -> none  [the longest x1 22 us: shards(): lax.all_to_all(send_tokens, 'expert', split_axis=0, concat_axis=0, tiled=...]
    dot_general x10 -> x0, matrix products: 14.9 us -> none  [the longest x1 3.49 us: shards(): gate_sum = jnp.dot(piece, gate_local, preferred_element_type=jnp.float32)]
    unnamed x22 -> x10, local copies, waits for them, and re-layouts: 14.1 us -> 6.07 us
  transfers between devices with their start and end apart: 6 -> 0, of which waited for: 5 -> 0; matrix products, arithmetic and copies ran while one was open for 5% -> 0% of each run, Pallas kernels for 0% -> 0%
where the time goes in v1:
time: 111 us; the launch traced here: 110 us
  Pallas kernels  103 us (93%)
  local copies, waits for them, and re-layouts  6.07 us (5%)
    pallas_call x1, Pallas kernels, shards(): pl.pallas_call(functools.partial(kernel, cap, nz), out_shape=(out, out),...  103 us
    unnamed x10, local copies, waits for them, and re-layouts  6.07 us

profile of v1, /device:TPU:1, one launch (start us, length us, event | category | flops | bytes accessed | tf_op | source)
XLA Modules:
  0.0 109.7 jit_solution(656742826584824112)
XLA Ops:
  0.6 0.8 copy.9.routes_ref
  1.4 0.8 copy.10.gates_ref
  2.2 0.0 copy-start
  2.2 1.9 %copy-done = bf16[1,4096,384]{2,1,0:T(8,128)(2,1)S(1)} copy-done((bf16[1,4096,384]{2,1,0:T(8,128)(2,1)S(1)}, bf16[1,4096,384]{2,1,0:T(8,128)(2,1)}, u32[]{:S(2)}) %copy-start) | copy-done | bytes 3145752
  4.1 0.0 copy-start.1
  4.1 0.7 copy-done.1
  4.8 0.0 copy-start.2
  4.8 0.7 copy-done.2
  5.5 103.0 %moe_layer.1 = (bf16[64,128]{1,0:T(8,128)(2,1)S(1)}, bf16[64,128]{1,0:T(8,128)(2,1)S(1)}) custom-call(bf16[64,128]{1,0:T(8,128)(2,1)S(1)} %copy-done.1, bf16[64,128]{1,0:T(8,128)(2,1)S(1)} %copy-done.2, s32[64,2]{1,0:T(8,128)S(1)} %copy.9.routes_ref, f32[64,2]{1,0:T(8,128)S(1)} %copy.10.gates_ref, bf16[1,4096,384]{2,1,0:T(8,128)(2,1)S(1)} %copy-done, ...), custom_call_target="tpu_custom_call" | custom-call | flops 7247757312 | bytes 9437184 | tf_op jit(solution)/shard_map/moe_layer/pallas_call | solution.py:443
  108.5 0.6 copy.13
  109.1 0.6 copy.14
Async XLA Ops:
  2.2 1.9 %copy-start = (bf16[1,4096,384]{2,1,0:T(8,128)(2,1)S(1)}, bf16[1,4096,384]{2,1,0:T(8,128)(2,1)}, u32[]{:S(2)}) copy-start(bf16[1,4096,384]{2,1,0:T(8,128)(2,1)} %wg_hbm.1) | copy-start | bytes 9437188
  4.1 0.7 copy-start.1
  4.8 0.7 copy-start.2

commit v2 on v1

--- a/solution.py
+++ b/solution.py
@@ -16,10 +16,10 @@
 def kernel(
     cap,
     nz,
-    tok_ref,
-    cot_ref,
-    routes_ref,
-    gates_ref,
+    tok_hbm,
+    cot_hbm,
+    routes_hbm,
+    gates_hbm,
     wg_hbm,
     wu_hbm,
     wd_hbm,
@@ -39,6 +39,9 @@
     qt_ref,
     gs_ref,
     pick_ref,
+    routes_ref,
+    gates_ref,
+    gate_cols,
     odd_out,
     odd_in,
     back,
@@ -61,7 +64,7 @@
 ):
     dp, me, z = lax.axis_index("dp"), lax.axis_index("expert"), lax.axis_index("tensor")
     ne = lax.axis_size("expert")
-    toks, cols = tok_ref.shape
+    toks, cols = tok_hbm.shape
     hidden = wd.shape[0]
     pair = 2 * cap
     rows = ne * pair
@@ -89,13 +92,35 @@
     greeted = [at_z(1), at_z(-1), at_z(2), at_z(-2)] + [peer(i) for i in range(1, ne)]
     for device in greeted:
         pl.semaphore_signal(barrier, inc=1, device_id=device, device_id_type=MESH)
-    for load in loads:
+    small = [
+        pltpu.make_async_copy(src, dst, w_sem.at[3 + i])
+        for i, (src, dst) in enumerate(
+            (
+                (routes_hbm, routes_ref),
+                (gates_hbm, gates_ref),
+                (tok_hbm, raw.at[0, pl.ds(0, toks)]),
+                (cot_hbm, raw.at[0, pl.ds(toks, toks)]),
+            )
+        )
+    ]
+    for load in small + loads:
         load.start()
-
-    raw[0, 0:toks, :] = tok_ref[...]
-    raw[0, toks : 2 * toks, :] = cot_ref[...]
+    for load in small:
+        load.wait()
+
+    square = lax.broadcasted_iota(jnp.int32, (toks, toks), 0) == lax.broadcasted_iota(
+        jnp.int32, (toks, toks), 1
+    )
+
+    def column_of(ref, k):
+        return jnp.sum(jnp.where(square, ref[k : k + 1, :].astype(F32), 0.0), axis=1, keepdims=True)
+
+    gate_col = [column_of(gates_ref, k) for k in range(2)]
+    route_col = [column_of(routes_ref, k) for k in range(2)]
+    for k in range(2):
+        gate_cols[k] = jnp.broadcast_to(gate_col[k], (toks, cols))
     lane = lax.broadcasted_iota(jnp.int32, (toks, 128), 1)
-    chosen = [(routes_ref[:, k : k + 1] == lane).astype(F32) for k in range(2)]
+    chosen = [(route_col[k] == lane.astype(F32)).astype(F32) for k in range(2)]
     before = (
         lax.broadcasted_iota(jnp.int32, (toks, toks), 1) < lax.broadcasted_iota(jnp.int32, (toks, toks), 0)
     ).astype(BF16)
@@ -118,7 +143,7 @@
     placing, scale = 0.0, 0.0
     for k in range(2):
         row_target = jnp.sum(jnp.where(diagonal, target[k], 0.0), axis=0, keepdims=True) + second
-        row_gate = jnp.sum(jnp.where(diagonal, gates_ref[:, k : k + 1], 0.0), axis=0, keepdims=True)
+        row_gate = jnp.sum(jnp.where(diagonal, gate_col[k], 0.0), axis=0, keepdims=True)
         row_gate = jnp.where(lanes1 < toks, 1.0, row_gate)
         hit = down_rows == row_target
         placing = placing + hit.astype(F32)
@@ -217,59 +242,71 @@
         for i in range(1, ne):
             y_copy(k, i, out, into, send, recv).wait_send()
 
+    def forward_next(k):
+        for d in range(2):
+            raw_copy(k + 1, d).start()
+
+    def forward_last():
+        for d in range(2):
+            raw_last(d).start()
+
+    def gather_step(k, forward):
+        for d in range(2):
+            raw_copy(k, d).wait_recv()
+        forward()
+        dispatch(k)
+        for d in range(2):
+            raw_copy(k, d).wait_send()
+
+    def settle(k):
+        for d in range(2):
+            odd_copy(k, d).wait_send()
+        y_sent(k, stage, even, y_s, y_r)
+
     for d in range(2):
         raw_copy(1, d).start()
     dispatch(0)
-    for d in range(2):
-        raw_copy(1, d).wait_recv()
-    for d in range(2):
-        raw_copy(2, d).start()
-    dispatch(1)
+    gather_step(1, lambda: forward_next(1))
+    gather_step(2, lambda: forward_next(2))
     pass_on(0)
     for load in loads:
         load.wait()
     accumulate([(even, 0, 0)], first=True)
-    for d in range(2):
-        raw_copy(1, d).wait_send()
-
-    def gather_step(k, forward):
-        for d in range(2):
-            raw_copy(k, d).wait_recv()
-        forward()
-        dispatch(k)
-        pass_on(k - 1)
-        odd_arrived(k - 2)
-        accumulate(even_parts(k - 1) + odd_parts(k - 2))
-        for d in range(2):
-            raw_copy(k, d).wait_send()
-            odd_copy(k - 2, d).wait_send()
-        y_sent(k - 2, stage, even, y_s, y_r)
-
-    def forward_next(k):
-        for d in range(2):
-            raw_copy(k + 1, d).start()
-
-    def forward_last():
-        for d in range(2):
-            raw_last(d).start()
-
-    gather_step(2, lambda: forward_next(2))
+    gather_step(3, lambda: forward_next(3))
+    pass_on(1)
+    accumulate(even_parts(1))
+
+    def gather_full(k):
+        gather_step(k, lambda: forward_next(k))
+        pass_on(k - 2)
+        odd_arrived(k - 4)
+        accumulate(even_parts(k - 2) + odd_parts(k - 4))
+        settle(k - 4)
 
     def gather_loop(k, carry):
-        gather_step(k, lambda: forward_next(k))
+        gather_full(k)
         return carry
 
-    lax.fori_loop(3, last - 1, gather_loop, 0)
+    gather_full(4)
+    lax.fori_loop(5, last - 1, gather_loop, 0)
     gather_step(last - 1, forward_last)
+    pass_on(last - 3)
+    odd_arrived(last - 5)
+    accumulate(even_parts(last - 3) + odd_parts(last - 5))
     for d in range(2):
         raw_last(d).wait_recv()
     dispatch(last)
+    pass_on(last - 2)
+    odd_arrived(last - 4)
+    accumulate(even_parts(last - 2) + odd_parts(last - 4))
     pass_on(last - 1)
+    odd_arrived(last - 3)
+    accumulate(even_parts(last - 1) + odd_parts(last - 3))
+    pass_on(last)
     odd_arrived(last - 2)
-    accumulate(even_parts(last - 1) + odd_parts(last - 2))
-    pass_on(last)
+    accumulate([(even, 2 * last - 1, 2 * last)] + odd_parts(last - 2))
     odd_arrived(last - 1)
-    accumulate([(even, 2 * last - 1, 2 * last)] + odd_parts(last - 1))
+    accumulate(odd_parts(last - 1))
 
     for j in range(ne // 2):
         top = 2 * pair * j
@@ -339,7 +376,10 @@
         if slices(k) == 2:
             block = jnp.concatenate([block, home[2 * k].reshape(rows, cols)], axis=1)
         picked = jnp.dot(pick_ref[...], block, preferred_element_type=F32)
-        mixed = gates_ref[:, 0:1] * picked[:toks] + gates_ref[:, 1:2] * picked[toks : 2 * toks]
+        g0, g1 = gate_cols[0], gate_cols[1]
+        if slices(k) == 2:
+            g0, g1 = jnp.concatenate([g0, g0], axis=1), jnp.concatenate([g1, g1], axis=1)
+        mixed = g0 * picked[:toks] + g1 * picked[toks : 2 * toks]
         return mixed, picked[2 * toks :]
 
     def chain_copy(k, d):
@@ -377,34 +417,38 @@
     send_even(last)
     send_odd(last - 2)
     send_even(last - 1)
+    send_odd(last - 3)
+    send_odd(last - 4)
+    send_even(last - 2)
     for d in range(2):
         raw_last(d).wait_send()
-        odd_copy(last - 2, d).wait_send()
-        odd_copy(last - 1, d).wait_send()
-    for k in (last - 2, last - 1, last):
-        y_sent(k, stage, even, y_s, y_r)
+    for k in range(last - 5, last):
+        settle(k)
+    y_sent(last, stage, even, y_s, y_r)
     mixed, grad = combine(last)
     chain_out[2 * last - 1, 0:toks, :] = mixed.astype(BF16)
     chain_out[2 * last - 1, toks : 2 * toks, :] = grad.astype(BF16)
     for d in range(2):
         chain_first(d).start()
-
-    send_odd(last - 3)
-    send_even(last - 2)
     chain_step(last - 1, halves=True)
+    send_odd(last - 5)
+    send_even(last - 3)
 
     def back_loop(n, carry):
-        k = last - 3 - n
-        send_odd(k - 1)
-        send_even(k)
-        chain_step(k + 1)
-        for d in range(2):
-            po_copy(k + 2, d).wait_send()
-            chain_copy(k + 2, d).wait_send()
-        y_sent(k + 2, back, home, b_s, b_r)
+        k = last - 2 - n
+        chain_step(k)
+        send_odd(k - 4)
+        send_even(k - 2)
+        for d in range(2):
+            po_copy(k + 1, d).wait_send()
+            chain_copy(k + 1, d).wait_send()
+        y_sent(k + 1, back, home, b_s, b_r)
         return carry
 
-    lax.fori_loop(0, last - 3, back_loop, 0)
+    lax.fori_loop(0, last - 5, back_loop, 0)
+    chain_step(3)
+    send_even(1)
+    chain_step(2)
     send_even(0)
     chain_step(1)
     mixed, grad = combine(0)
@@ -416,11 +460,11 @@
     grad_ref[...] = grad.astype(BF16)
     for d in range(2):
         chain_first(d).wait_send()
-        for k in (2, 1):
+        for k in (4, 3, 2, 1):
             chain_copy(k, d).wait_send()
-        for k in (2, 1, 0):
+        for k in (4, 3, 2, 1, 0):
             po_copy(k, d).wait_send()
-    for k in (last, 2, 1, 0):
+    for k in (last, 4, 3, 2, 1, 0):
         y_sent(k, back, home, b_s, b_r)
 
 
@@ -443,7 +487,7 @@
     return pl.pallas_call(
         functools.partial(kernel, cap, nz),
         out_shape=(out, out),
-        in_specs=[vmem] * 4 + [anywhere] * 3,
+        in_specs=[anywhere] * 7,
         out_specs=(vmem, vmem),
         scratch_shapes=[
             pltpu.VMEM((width, hidden), BF16),
@@ -460,13 +504,16 @@
             pltpu.VMEM((rows, 2 * toks), BF16),
             pltpu.VMEM((rows, 128), F32),
             pltpu.VMEM((3 * toks, rows), BF16),
+            pltpu.VMEM((2, toks), jnp.int32),
+            pltpu.VMEM((2, toks), F32),
+            pltpu.VMEM((2, toks, cols), F32),
             flat,
             flat,
             staged,
             slab,
             pltpu.VMEM((half, 2 * toks, cols), BF16),
             pltpu.VMEM((half, 2 * toks, cols), BF16),
-            dma((3,)),
+            dma((7,)),
             dma((half + 1,)),
             dma((half + 1,)),
             dma((steps, ne)),
@@ -485,9 +532,9 @@
             flops=12 * rows * width * hidden, bytes_accessed=6 * width * hidden, transcendentals=rows * hidden
         ),
         compiler_params=pltpu.CompilerParams(
-            collective_id=0, has_side_effects=True, vmem_limit_bytes=48 * 1024 * 1024
+            collective_id=0, has_side_effects=True, vmem_limit_bytes=60 * 1024 * 1024
         ),
-    )(tokens, cotangent, routes, gates, w_gate, w_up, w_down)
+    )(tokens, cotangent, routes.T, gates.T, w_gate, w_up, w_down)
 
 
 def solution(mesh):

time: 111 us -> 110 us (level)
  the two profiles are of different devices: /device:TPU:1 before, /device:TPU:2 now
where the time goes in v2:
time: 110 us; the launch traced here: 109 us
  Pallas kernels  106 us (96%)
  local copies, waits for them, and re-layouts  2.65 us (2%)
    pallas_call x1, Pallas kernels, shards(): pl.pallas_call(functools.partial(kernel, cap, nz), out_shape=(out, out),...  106 us
    unnamed x2, local copies, waits for them, and re-layouts  2.65 us

profile of v2, /device:TPU:2, one launch (start us, length us, event | category | flops | bytes accessed | tf_op | source)
XLA Modules:
  0.0 109.2 jit_solution(5288020447834259946)
XLA Ops:
  0.6 105.9 %moe_layer.1 = (bf16[64,128]{1,0:T(8,128)(2,1)}, bf16[64,128]{1,0:T(8,128)(2,1)}) custom-call(bf16[64,128]{1,0:T(8,128)(2,1)} %tok_hbm.1, bf16[64,128]{1,0:T(8,128)(2,1)} %cot_hbm.1, s32[2,64]{1,0:T(2,128)} %bitcast.2, f32[2,64]{1,0:T(2,128)} %bitcast.3, bf16[1,4096,384]{2,1,0:T(8,128)(2,1)} %wg_hbm.1, bf16[1,4096,384]{2,1,0:T(8,128)(2,1)} %wu_hbm.1, ...), custom_call_target="tpu_custom_call" | custom-call | flops 7247757312 | bytes 9437184 | tf_op jit(solution)/shard_map/moe_layer/pallas_call | solution.py:487
  106.5 1.3 %copy.11 = bf16[64,128]{1,0:T(8,128)(2,1)} copy(bf16[64,128]{1,0:T(8,128)(2,1)} %get-tuple-element.4) | data formatting | bytes 32768
  107.9 1.3 %copy.12 = bf16[64,128]{1,0:T(8,128)(2,1)} copy(bf16[64,128]{1,0:T(8,128)(2,1)} %get-tuple-element.5) | data formatting | bytes 32768

commit v3 on v2

v3 whole, which is shorter than its diff:
```python
import functools

import jax
import jax.numpy as jnp
from jax import lax
from jax.experimental import pallas as pl
from jax.experimental.pallas import tpu as pltpu
from jax.sharding import PartitionSpec as P

MESH = pl.DeviceIdType.MESH
F32 = jnp.float32
BF16 = jnp.bfloat16
NT = (((1,), (1,)), ((), ()))


def kernel(
    cap,
    nz,
    tok_hbm,
    cot_hbm,
    routes_hbm,
    gates_hbm,
    wg_hbm,
    wu_hbm,
    wd_hbm,
    mixed_ref,
    grad_ref,
    wg,
    wu,
    wd,
    raw,
    stage,
    slots,
    odd,
    acc,
    hid,
    gg,
    gu,
    qt_ref,
    gs_ref,
    pick_ref,
    routes_ref,
    gates_ref,
    gate_cols,
    odd_out,
    odd_in,
    back,
    home,
    fill_out,
    fill_in,
    far_in,
    chain_out,
    chain_in,
    w_sem,
    raw_s,
    raw_r,
    y_s,
    y_r,
    odd_s,
    odd_r,
    po_s,
    po_r,
    b_s,
    b_r,
    f_s,
    f_r,
    c_s,
    c_r,
):
    dp, me, z = lax.axis_index("dp"), lax.axis_index("expert"), lax.axis_index("tensor")
    ne = lax.axis_size("expert")
    toks, cols = tok_hbm.shape
    hidden = wd.shape[0]
    pair = 2 * cap
    rows = ne * pair
    hop = 3
    last = (nz // 2 - 1) // hop

    def at_z(offset):
        return (dp, me, lax.rem(z + offset + nz, nz))

    def peer(i):
        return (dp, lax.rem(me + i, ne), z)

    def remote(src, dst, send, recv, device):
        return pltpu.make_async_remote_copy(
            src_ref=src, dst_ref=dst, send_sem=send, recv_sem=recv, device_id=device, device_id_type=MESH
        )

    def feat(offset):
        return pl.ds(pl.multiple_of(lax.rem(z + offset + nz, nz) * cols, cols), cols)

    def places(j):
        return {0: (0, 1), 1: (0, 2), last + 1: (1, 3)}.get(j, (0, 4))

    def offset(j, s):
        if j == last + 1 and s == 1:
            return nz // 2
        return (1 if s % 2 else -1) * (hop * j if s < 2 else hop * j - 4)

    def joined(blocks, axis):
        return blocks[0] if len(blocks) == 1 else jnp.concatenate(blocks, axis=axis)

    loads = [
        pltpu.make_async_copy(src, dst, w_sem.at[i])
        for i, (src, dst) in enumerate(((wg_hbm.at[0], wg), (wu_hbm.at[0], wu), (wd_hbm.at[0], wd)))
    ]
    barrier = pltpu.get_barrier_semaphore()
    greeted = [at_z(1), at_z(-1), at_z(hop), at_z(-hop)] + [peer(i) for i in range(1, ne)]
    for device in greeted:
        pl.semaphore_signal(barrier, inc=1, device_id=device, device_id_type=MESH)
    small = [
        pltpu.make_async_copy(src, dst, w_sem.at[3 + i])
        for i, (src, dst) in enumerate(
            (
                (routes_hbm, routes_ref),
                (gates_hbm, gates_ref),
                (tok_hbm, raw.at[0, 0, pl.ds(0, toks)]),
                (cot_hbm, raw.at[0, 0, pl.ds(toks, toks)]),
            )
        )
    ]
    for load in small + loads:
        load.start()
    for load in small:
        load.wait()
    pl.semaphore_wait(barrier, len(greeted))

    def raw_copy(j, d):
        i = 2 * (j - 1) + d
        src = raw.at[0, 0] if j == 1 else raw.at[j - 1, d]
        return remote(src, raw.at[j, d], raw_s.at[i], raw_r.at[i], at_z(hop - 2 * hop * d))

    def fill_copy(j, d):
        i = 2 * last + 2 * (j - 1) + d
        return remote(raw.at[j, d], raw.at[j + 1, 2 + d], raw_s.at[i], raw_r.at[i], at_z(2 * d - 1))

    def far_copy(d):
        i = 4 * last + d
        part = pl.ds(d * toks, toks)
        return remote(raw.at[last, d, part], raw.at[last + 1, 1, part], raw_s.at[i], raw_r.at[i], at_z(1 - 2 * d))

    def exchange(j, out, into, send, recv):
        a, n = places(j)
        for i in range(1, ne):
            to = lax.rem(me + i, ne)
            remote(
                out.at[j, to, pl.ds(a, n)], into.at[j, pl.ds(a, n), me], send.at[j], recv.at[j], peer(i)
            ).start()
        for s in range(a, a + n):
            into[j, s, me] = out[j, me, s]

    def exchanged(j, into, send, recv):
        a, n = places(j)
        every = into.at[j, pl.ds(a, n), pl.ds(0, ne - 1)]
        return remote(every, every, send.at[j], recv.at[j], peer(1))

    def dispatch(j):
        a, n = places(j)
        block = joined([raw[j, s] for s in range(a, a + n)], 1)
        placed = jnp.dot(qt_ref[...], block, preferred_element_type=F32)
        for s in range(n):
            one = (placed[:, s * cols : (s + 1) * cols] * gs_ref[...]).astype(BF16)
            stage[j, :, a + s] = one.reshape(ne, pair, cols)
        exchange(j, stage, slots, y_s, y_r)

    def odd_copy(j, d):
        i = 2 * j + d
        src = slots.at[0, 0] if j == 0 else slots.at[j, d]
        return remote(src, odd.at[j, d], odd_s.at[i], odd_r.at[i], at_z(1 - 2 * d))

    def pass_on(j):
        exchanged(j, slots, y_s, y_r).wait_recv()
        if j < last:
            for d in range(2):
                odd_copy(j, d).start()

    def accumulate(j, o):
        parts = []
        if j is not None:
            a, n = places(j)
            parts += [(slots[j, s], offset(j, s)) for s in range(a, a + n)]
        if o >= 0:
            for d in range(2):
                odd_copy(o, d).wait_recv()
                parts.append((odd[o, d], (2 * d - 1) * (hop * o + 1)))
        lhs = joined([block.reshape(rows, cols) for block, _ in parts], 1)
        for n, w in enumerate((wg, wu, wd)):
            if n < 2:
                rhs = joined([w[feat(x), :] for _, x in parts], 0)
                term = jnp.dot(lhs, rhs, preferred_element_type=F32)
            else:
                rhs = joined([w[:, feat(x)] for _, x in parts], 1)
                term = lax.dot_general(lhs, rhs, NT, preferred_element_type=F32)
            span = slice(n * hidden, (n + 1) * hidden)
            if j == 0:
                acc[:, span] = term
            else:
                acc[:, span] += term

    for d in range(2):
        raw_copy(1, d).start()

    square = lax.broadcasted_iota(jnp.int32, (toks, toks), 0) == lax.broadcasted_iota(
        jnp.int32, (toks, toks), 1
    )

    def column_of(ref, k):
        return jnp.sum(jnp.where(square, ref[k : k + 1, :].astype(F32), 0.0), axis=1, keepdims=True)

    gate_col = [column_of(gates_ref, k) for k in range(2)]
    route_col = [column_of(routes_ref, k) for k in range(2)]
    for k in range(2):
        gate_cols[k] = jnp.broadcast_to(gate_col[k], (toks, cols))
    lane = lax.broadcasted_iota(jnp.int32, (toks, 128), 1)
    chosen = [(route_col[k] == lane.astype(F32)).astype(F32) for k in range(2)]
    before = (
        lax.broadcasted_iota(jnp.int32, (toks, toks), 1) < lax.broadcasted_iota(jnp.int32, (toks, toks), 0)
    ).astype(BF16)
    counts = jnp.dot(before, (chosen[0] + chosen[1]).astype(BF16), preferred_element_type=F32)
    target = [
        jnp.sum(chosen[k] * (counts + (lane * pair).astype(F32)), axis=1, keepdims=True) for k in range(2)
    ]
    wide = lax.broadcasted_iota(jnp.int32, (toks, rows), 1).astype(F32)
    for k in range(2):
        pick_ref[k * toks : (k + 1) * toks, :] = (wide == target[k]).astype(BF16)
    pick_ref[2 * toks : 3 * toks, :] = (
        (wide == target[0] + cap).astype(F32) + (wide == target[1] + cap).astype(F32)
    ).astype(BF16)
    token = lax.broadcasted_iota(jnp.int32, (toks, 2 * toks), 0)
    column = lax.broadcasted_iota(jnp.int32, (toks, 2 * toks), 1)
    diagonal = (column == token) | (column == token + toks)
    down_rows = lax.broadcasted_iota(jnp.int32, (rows, 2 * toks), 0).astype(F32)
    lanes1 = lax.broadcasted_iota(jnp.int32, (1, 2 * toks), 1)
    second = jnp.where(lanes1 < toks, 0.0, float(cap))
    placing, scale = 0.0, 0.0
    for k in range(2):
        row_target = jnp.sum(jnp.where(diagonal, target[k], 0.0), axis=0, keepdims=True) + second
        row_gate = jnp.sum(jnp.where(diagonal, gate_col[k], 0.0), axis=0, keepdims=True)
        row_gate = jnp.where(lanes1 < toks, 1.0, row_gate)
        hit = down_rows == row_target
        placing = placing + hit.astype(F32)
        scale = scale + jnp.sum(jnp.where(hit, row_gate, 0.0), axis=1, keepdims=True)
    qt_ref[...] = placing.astype(BF16)
    gs_ref[...] = jnp.broadcast_to(scale, (rows, 128))

    dispatch(0)
    for j in range(1, last + 1):
        for d in range(2):
            raw_copy(j, d).wait_recv()
            if j < last:
                raw_copy(j + 1, d).start()
            else:
                far_copy(d).start()
            fill_copy(j, d).start()
        if j > 1:
            for d in range(2):
                fill_copy(j - 1, d).wait_recv()
        dispatch(j)
        pass_on(j - 1)
        if j == 1:
            for load in loads:
                load.wait()
        accumulate(j - 1, j - 3)
        for d in range(2):
            raw_copy(j, d).wait_send()
    for d in range(2):
        fill_copy(last, d).wait_recv()
        far_copy(d).wait_recv()
    dispatch(last + 1)
    pass_on(last)
    accumulate(last, last - 2)
    pass_on(last + 1)
    accumulate(last + 1, last - 1)

    for j in range(ne // 2):
        top = 2 * pair * j
        mine = jnp.concatenate([acc[top : top + cap, :], acc[top + pair : top + pair + cap, :]], axis=0)
        gh = jnp.concatenate(
            [acc[top + cap : top + pair, 2 * hidden :], acc[top + pair + cap : top + 2 * pair, 2 * hidden :]],
            axis=0,
        )
        gate, up = mine[:, :hidden], mine[:, hidden : 2 * hidden]
        sigmoid = jax.nn.sigmoid(gate)
        active = gate * sigmoid
        span = slice(pair * j, pair * (j + 1))
        hid[span, :] = (active * up).astype(BF16)
        gg[span, :] = (gh * up * sigmoid * (1.0 + gate * (1.0 - sigmoid))).astype(BF16)
        gu[span, :] = (gh * active).astype(BF16)

    def partial(offsets):
        down = joined([wd[:, feat(o)] for o in offsets], 1)
        gate = joined([wg[feat(o), :] for o in offsets], 0)
        up = joined([wu[feat(o), :] for o in offsets], 0)
        out = jnp.dot(hid[...], down, preferred_element_type=F32)
        grad = lax.dot_general(gg[...], gate, NT, preferred_element_type=F32)
        grad = grad + lax.dot_general(gu[...], up, NT, preferred_element_type=F32)
        parts = []
        for e in range(ne):
            parts += [out[cap * e : cap * (e + 1)], grad[cap * e : cap * (e + 1)]]
        both = jnp.concatenate(parts, axis=0)
        return [both[:, s * cols : (s + 1) * cols] for s in range(len(offsets))]

    def po_copy(j, d):
        i = 2 * j + d
        return remote(odd_out.at[j, d], odd_in.at[j, d], po_s.at[i], po_r.at[i], at_z(2 * d - 1))

    def send_odd(j):
        for d, block in enumerate(partial([-hop * j - 1, hop * j + 1])):
            odd_out[j, d] = block.astype(BF16)
            po_copy(j, d).start()

    def send_group(j):
        a, n = places(j)
        total = partial([offset(j, s) for s in range(a, a + n)])
        if j < last:
            for d in range(2):
                po_copy(j, d).wait_recv()
                to = 0 if j == 0 else d
                total[to] = total[to] + odd_in[j, d].astype(F32)
        for s in range(n):
            back[j, :, a + s] = total[s].astype(BF16).reshape(ne, pair, cols)
        exchange(j, back, home, b_s, b_r)

    def back_fill(j, d):
        i = 2 * (j - 1) + d
        return remote(fill_out.at[j, d], fill_in.at[j, d], f_s.at[i], f_r.at[i], at_z(1 - 2 * d))

    def back_far(d):
        i = 2 * last + d
        part = pl.ds(d * toks, toks)
        return remote(fill_out.at[0, 0, part], far_in.at[part], f_s.at[i], f_r.at[i], at_z(2 * d - 1))

    def chain_copy(j, d):
        i = 2 * (j - 1) + d
        return remote(chain_out.at[j, d], chain_in.at[j - 1, d], c_s.at[i], c_r.at[i], at_z(2 * hop * d - hop))

    def combine(j):
        a, n = places(j)
        exchanged(j, home, b_s, b_r).wait_recv()
        block = joined([home[j, s].reshape(rows, cols) for s in range(a, a + n)], 1)
        picked = jnp.dot(pick_ref[...], block, preferred_element_type=F32)
        sums = [None] * 4
        for s in range(n):
            one = picked[:, s * cols : (s + 1) * cols]
            mixed = gate_cols[0] * one[:toks] + gate_cols[1] * one[toks : 2 * toks]
            sums[a + s] = jnp.concatenate([mixed, one[2 * toks :]], axis=0)
        if j > 1:
            for d in range(2):
                fill_out[j - 1, d] = sums[2 + d].astype(BF16)
                back_fill(j - 1, d).start()
        if j == last + 1:
            fill_out[0, 0] = sums[1].astype(BF16)
            for d in range(2):
                back_far(d).start()
        return sums

    def chain_step(j):
        sums = combine(j)
        for d in range(2):
            back_fill(j, d).wait_recv()
            total = sums[d] + fill_in[j, d].astype(F32)
            if j == last:
                back_far(d).wait_recv()
                half = far_in[d * toks : (d + 1) * toks, :].astype(F32)
                none = jnp.zeros_like(half)
                total = total + jnp.concatenate([half, none] if d == 0 else [none, half], axis=0)
            else:
                chain_copy(j + 1, d).wait_recv()
                total = total + chain_in[j, d].astype(F32)
            chain_out[j, d] = total.astype(BF16)
            chain_copy(j, d).start()

    send_group(last + 1)
    send_odd(last - 1)
    send_group(last)
    send_odd(last - 2)
    combine(last + 1)
    send_group(last - 1)
    send_odd(last - 3)
    chain_step(last)
    for j in range(last - 2, 0, -1):
        send_group(j)
        if j > 1:
            send_odd(j - 2)
        chain_step(j + 1)
    send_group(0)
    chain_step(1)
    sums = combine(0)[0]
    for d in range(2):
        for j in range(1, last + 1):
            fill_copy(j, d).wait_send()
            back_fill(j, d).wait_send()
            chain_copy(j, d).wait_send()
        far_copy(d).wait_send()
        back_far(d).wait_send()
        for j in range(last):
            odd_copy(j, d).wait_send()
            po_copy(j, d).wait_send()
    for j in range(last + 2):
        exchanged(j, slots, y_s, y_r).wait_send()
        exchanged(j, home, b_s, b_r).wait_send()
    for d in range(2):
        chain_copy(1, d).wait_recv()
        sums = sums + chain_in[0, d].astype(F32)
    mixed_ref[...] = sums[:toks].astype(BF16)
    grad_ref[...] = sums[toks:].astype(BF16)


def shards(tokens, cotangent, routes, gates, w_gate, w_up, w_down):
    ne, nz = lax.axis_size("expert"), lax.axis_size("tensor")
    toks, cols = tokens.shape
    width, hidden = w_gate.shape[1:]
    cap = toks * routes.shape[1] * 3 // (2 * ne)
    pair = 2 * cap
    rows = ne * pair
    last = (nz // 2 - 1) // 3
    groups = last + 2
    vmem = pl.BlockSpec(memory_space=pltpu.VMEM)
    hbm = pl.BlockSpec(memory_space=pl.ANY)
    dma = pltpu.SemaphoreType.DMA
    out = jax.ShapeDtypeStruct((toks, cols), BF16)
    staged = pltpu.VMEM((groups, ne, 4, pair, cols), BF16)
    landed = pltpu.VMEM((groups, 4, ne, pair, cols), BF16)
    flat = pltpu.VMEM((last, 2, rows, cols), BF16)
    tokens_of = pltpu.VMEM((last + 1, 2, 2 * toks, cols), BF16)
    return pl.pallas_call(
        functools.partial(kernel, cap, nz),
        out_shape=(out, out),
        in_specs=[hbm] * 7,
        out_specs=(vmem, vmem),
        scratch_shapes=[
            pltpu.VMEM((width, hidden), BF16),
            pltpu.VMEM((width, hidden), BF16),
            pltpu.VMEM((hidden, width), BF16),
            pltpu.VMEM((groups, 4, 2 * toks, cols), BF16),
            staged,
            landed,
            pltpu.VMEM((last, 2, ne, pair, cols), BF16),
            pltpu.VMEM((rows, 3 * hidden), F32),
            pltpu.VMEM((rows // 2, hidden), BF16),
            pltpu.VMEM((rows // 2, hidden), BF16),
            pltpu.VMEM((rows // 2, hidden), BF16),
            pltpu.VMEM((rows, 2 * toks), BF16),
            pltpu.VMEM((rows, 128), F32),
            pltpu.VMEM((3 * toks, rows), BF16),
            pltpu.VMEM((2, toks), jnp.int32),
            pltpu.VMEM((2, toks), F32),
            pltpu.VMEM((2, toks, cols), F32),
            flat,
            flat,
            staged,
            landed,
            tokens_of,
            tokens_of,
            pltpu.VMEM((2 * toks, cols), BF16),
            tokens_of,
            tokens_of,
            dma((7,)),
            dma((4 * last + 2,)),
            dma((4 * last + 2,)),
            dma((groups,)),
            dma((groups,)),
            dma((2 * last,)),
            dma((2 * last,)),
            dma((2 * last,)),
            dma((2 * last,)),
            dma((groups,)),
            dma((groups,)),
            dma((2 * last + 2,)),
            dma((2 * last + 2,)),
            dma((2 * last,)),
            dma((2 * last,)),
        ],
        name="moe_layer",
        cost_estimate=pl.CostEstimate(
            flops=12 * rows * width * hidden, bytes_accessed=6 * width * hidden, transcendentals=rows * hidden
        ),
        compiler_params=pltpu.CompilerParams(
            collective_id=0, has_side_effects=True, vmem_limit_bytes=60 * 1024 * 1024
        ),
    )(tokens, cotangent, routes.T, gates.T, w_gate, w_up, w_down)


def solution(mesh):
    return jax.shard_map(
        shards,
        mesh=mesh,
        in_specs=(
            P(("dp", "expert"), "tensor"),
            P(("dp", "expert"), "tensor"),
            P(("dp", "expert"), None),
            P(("dp", "expert"), None),
            P("expert", None, "tensor"),
            P("expert", None, "tensor"),
            P("expert", "tensor", None),
        ),
        out_specs=(P(("dp", "expert"), "tensor"), P(("dp", "expert"), "tensor")),
        check_vma=False,
    )
```

time: 110 us -> 99.7 us (0.906)
  the two profiles are of different devices: /device:TPU:2 before, /device:TPU:1 now
where the time goes in v3:
time: 99.7 us; the launch traced here: 98.6 us
  Pallas kernels  95.3 us (96%)
  local copies, waits for them, and re-layouts  2.65 us (3%)
    pallas_call x1, Pallas kernels, shards(): pl.pallas_call(functools.partial(kernel, cap, nz), out_shape=(out, out),...  95.3 us
    unnamed x2, local copies, waits for them, and re-layouts  2.65 us

profile of v3, /device:TPU:1, one launch (start us, length us, event | category | flops | bytes accessed | tf_op | source)
XLA Modules:
  0.0 98.6 jit_solution(10523758654407509418)
XLA Ops:
  0.6 95.3 %moe_layer.1 = (bf16[64,128]{1,0:T(8,128)(2,1)}, bf16[64,128]{1,0:T(8,128)(2,1)}) custom-call(bf16[64,128]{1,0:T(8,128)(2,1)} %tok_hbm.1, bf16[64,128]{1,0:T(8,128)(2,1)} %cot_hbm.1, s32[2,64]{1,0:T(2,128)} %bitcast.2, f32[2,64]{1,0:T(2,128)} %bitcast.3, bf16[1,4096,384]{2,1,0:T(8,128)(2,1)} %wg_hbm.1, bf16[1,4096,384]{2,1,0:T(8,128)(2,1)} %wu_hbm.1, ...), custom_call_target="tpu_custom_call" | custom-call | flops 7247757312 | bytes 9437184 | tf_op jit(solution)/shard_map/moe_layer/pallas_call | solution.py:427
  96.0 1.3 %copy.11 = bf16[64,128]{1,0:T(8,128)(2,1)} copy(bf16[64,128]{1,0:T(8,128)(2,1)} %get-tuple-element.4) | data formatting | bytes 32768
  97.3 1.3 %copy.12 = bf16[64,128]{1,0:T(8,128)(2,1)} copy(bf16[64,128]{1,0:T(8,128)(2,1)} %get-tuple-element.5) | data formatting | bytes 32768

commit v4 on v3

--- a/solution.py
+++ b/solution.py
@@ -23,8 +23,7 @@
     wg_hbm,
     wu_hbm,
     wd_hbm,
-    mixed_ref,
-    grad_ref,
+    out_ref,
     wg,
     wu,
     wd,
@@ -91,12 +90,12 @@
         return pl.ds(pl.multiple_of(lax.rem(z + offset + nz, nz) * cols, cols), cols)
 
     def places(j):
-        return {0: (0, 1), 1: (0, 2), last + 1: (1, 3)}.get(j, (0, 4))
+        return {0: (0, 1), last: (0, 2), last + 1: (1, 3)}.get(j, (0, 4))
 
     def offset(j, s):
         if j == last + 1 and s == 1:
             return nz // 2
-        return (1 if s % 2 else -1) * (hop * j if s < 2 else hop * j - 4)
+        return (1 if s % 2 else -1) * (hop * j if s < 2 else hop * min(j, last) - 1)
 
     def joined(blocks, axis):
         return blocks[0] if len(blocks) == 1 else jnp.concatenate(blocks, axis=axis)
@@ -106,7 +105,7 @@
         for i, (src, dst) in enumerate(((wg_hbm.at[0], wg), (wu_hbm.at[0], wu), (wd_hbm.at[0], wd)))
     ]
     barrier = pltpu.get_barrier_semaphore()
-    greeted = [at_z(1), at_z(-1), at_z(hop), at_z(-hop)] + [peer(i) for i in range(1, ne)]
+    greeted = [at_z(sign * n) for n in (1, 2, hop, 4) for sign in (1, -1)] + [peer(i) for i in range(1, ne)]
     for device in greeted:
         pl.semaphore_signal(barrier, inc=1, device_id=device, device_id_type=MESH)
     small = [
@@ -131,14 +130,20 @@
         src = raw.at[0, 0] if j == 1 else raw.at[j - 1, d]
         return remote(src, raw.at[j, d], raw_s.at[i], raw_r.at[i], at_z(hop - 2 * hop * d))
 
+    def filled(j):
+        return j + 1 if j < last - 1 else last + 1
+
     def fill_copy(j, d):
-        i = 2 * last + 2 * (j - 1) + d
-        return remote(raw.at[j, d], raw.at[j + 1, 2 + d], raw_s.at[i], raw_r.at[i], at_z(2 * d - 1))
+        i = 2 * last + 2 * j + d
+        src = raw.at[0, 0] if j == 0 else raw.at[j, d]
+        return remote(src, raw.at[filled(j), 2 + d], raw_s.at[i], raw_r.at[i], at_z(2 - 4 * d))
 
     def far_copy(d):
         i = 4 * last + d
         part = pl.ds(d * toks, toks)
-        return remote(raw.at[last, d, part], raw.at[last + 1, 1, part], raw_s.at[i], raw_r.at[i], at_z(1 - 2 * d))
+        return remote(
+            raw.at[last - 1, d, part], raw.at[last + 1, 1, part], raw_s.at[i], raw_r.at[i], at_z(4 - 8 * d)
+        )
 
     def exchange(j, out, into, send, recv):
         a, n = places(j)
@@ -200,6 +205,7 @@
 
     for d in range(2):
         raw_copy(1, d).start()
+        fill_copy(0, d).start()
 
     square = lax.broadcasted_iota(jnp.int32, (toks, toks), 0) == lax.broadcasted_iota(
         jnp.int32, (toks, toks), 1
@@ -245,17 +251,15 @@
     gs_ref[...] = jnp.broadcast_to(scale, (rows, 128))
 
     dispatch(0)
-    for j in range(1, last + 1):
+    for j in range(1, last):
         for d in range(2):
             raw_copy(j, d).wait_recv()
-            if j < last:
-                raw_copy(j + 1, d).start()
-            else:
+            raw_copy(j + 1, d).start()
+            fill_copy(j, d).start()
+            if j == last - 1:
                 far_copy(d).start()
-            fill_copy(j, d).start()
-        if j > 1:
-            for d in range(2):
-                fill_copy(j - 1, d).wait_recv()
+        for d in range(2):
+            fill_copy(j - 1, d).wait_recv()
         dispatch(j)
         pass_on(j - 1)
         if j == 1:
@@ -265,9 +269,14 @@
         for d in range(2):
             raw_copy(j, d).wait_send()
     for d in range(2):
-        fill_copy(last, d).wait_recv()
+        raw_copy(last, d).wait_recv()
+    dispatch(last)
+    for d in range(2):
+        fill_copy(last - 1, d).wait_recv()
         far_copy(d).wait_recv()
     dispatch(last + 1)
+    pass_on(last - 1)
+    accumulate(last - 1, last - 3)
     pass_on(last)
     accumulate(last, last - 2)
     pass_on(last + 1)
@@ -323,13 +332,13 @@
         exchange(j, back, home, b_s, b_r)
 
     def back_fill(j, d):
-        i = 2 * (j - 1) + d
-        return remote(fill_out.at[j, d], fill_in.at[j, d], f_s.at[i], f_r.at[i], at_z(1 - 2 * d))
+        i = 2 * j + d
+        return remote(fill_out.at[j, d], fill_in.at[j, d], f_s.at[i], f_r.at[i], at_z(4 * d - 2))
 
     def back_far(d):
         i = 2 * last + d
         part = pl.ds(d * toks, toks)
-        return remote(fill_out.at[0, 0, part], far_in.at[part], f_s.at[i], f_r.at[i], at_z(2 * d - 1))
+        return remote(fill_out.at[last, 0, part], far_in.at[part], f_s.at[i], f_r.at[i], at_z(8 * d - 4))
 
     def chain_copy(j, d):
         i = 2 * (j - 1) + d
@@ -345,12 +354,13 @@
             one = picked[:, s * cols : (s + 1) * cols]
             mixed = gate_cols[0] * one[:toks] + gate_cols[1] * one[toks : 2 * toks]
             sums[a + s] = jnp.concatenate([mixed, one[2 * toks :]], axis=0)
-        if j > 1:
-            for d in range(2):
-                fill_out[j - 1, d] = sums[2 + d].astype(BF16)
-                back_fill(j - 1, d).start()
+        for place in range(last):
+            if filled(place) == j:
+                for d in range(2):
+                    fill_out[place, d] = sums[2 + d].astype(BF16)
+                    back_fill(place, d).start()
         if j == last + 1:
-            fill_out[0, 0] = sums[1].astype(BF16)
+            fill_out[last, 0] = sums[1].astype(BF16)
             for d in range(2):
                 back_far(d).start()
         return sums
@@ -358,27 +368,27 @@
     def chain_step(j):
         sums = combine(j)
         for d in range(2):
-            back_fill(j, d).wait_recv()
-            total = sums[d] + fill_in[j, d].astype(F32)
-            if j == last:
+            total = sums[d]
+            if j < last:
+                back_fill(j, d).wait_recv()
+                chain_copy(j + 1, d).wait_recv()
+                total = total + fill_in[j, d].astype(F32) + chain_in[j, d].astype(F32)
+            if j == last - 1:
                 back_far(d).wait_recv()
                 half = far_in[d * toks : (d + 1) * toks, :].astype(F32)
                 none = jnp.zeros_like(half)
                 total = total + jnp.concatenate([half, none] if d == 0 else [none, half], axis=0)
-            else:
-                chain_copy(j + 1, d).wait_recv()
-                total = total + chain_in[j, d].astype(F32)
             chain_out[j, d] = total.astype(BF16)
             chain_copy(j, d).start()
 
+    send_group(last)
     send_group(last + 1)
     send_odd(last - 1)
-    send_group(last)
     send_odd(last - 2)
+    chain_step(last)
     combine(last + 1)
     send_group(last - 1)
     send_odd(last - 3)
-    chain_step(last)
     for j in range(last - 2, 0, -1):
         send_group(j)
         if j > 1:
@@ -389,9 +399,10 @@
     sums = combine(0)[0]
     for d in range(2):
         for j in range(1, last + 1):
-            fill_copy(j, d).wait_send()
-            back_fill(j, d).wait_send()
+            fill_copy(j - 1, d).wait_send()
+            back_fill(j - 1, d).wait_send()
             chain_copy(j, d).wait_send()
+        raw_copy(last, d).wait_send()
         far_copy(d).wait_send()
         back_far(d).wait_send()
         for j in range(last):
@@ -401,10 +412,11 @@
         exchanged(j, slots, y_s, y_r).wait_send()
         exchanged(j, home, b_s, b_r).wait_send()
     for d in range(2):
+        back_fill(0, d).wait_recv()
         chain_copy(1, d).wait_recv()
-        sums = sums + chain_in[0, d].astype(F32)
-    mixed_ref[...] = sums[:toks].astype(BF16)
-    grad_ref[...] = sums[toks:].astype(BF16)
+        sums = sums + fill_in[0, d].astype(F32) + chain_in[0, d].astype(F32)
+    out_ref[0] = sums[:toks].astype(BF16)
+    out_ref[1] = sums[toks:].astype(BF16)
 
 
 def shards(tokens, cotangent, routes, gates, w_gate, w_up, w_down):
@@ -419,16 +431,16 @@
     vmem = pl.BlockSpec(memory_space=pltpu.VMEM)
     hbm = pl.BlockSpec(memory_space=pl.ANY)
     dma = pltpu.SemaphoreType.DMA
-    out = jax.ShapeDtypeStruct((toks, cols), BF16)
+    out = jax.ShapeDtypeStruct((2, toks, cols), BF16)
     staged = pltpu.VMEM((groups, ne, 4, pair, cols), BF16)
     landed = pltpu.VMEM((groups, 4, ne, pair, cols), BF16)
     flat = pltpu.VMEM((last, 2, rows, cols), BF16)
     tokens_of = pltpu.VMEM((last + 1, 2, 2 * toks, cols), BF16)
-    return pl.pallas_call(
+    both = pl.pallas_call(
         functools.partial(kernel, cap, nz),
-        out_shape=(out, out),
+        out_shape=out,
         in_specs=[hbm] * 7,
-        out_specs=(vmem, vmem),
+        out_specs=vmem,
         scratch_shapes=[
             pltpu.VMEM((width, hidden), BF16),
             pltpu.VMEM((width, hidden), BF16),
@@ -480,6 +492,7 @@
             collective_id=0, has_side_effects=True, vmem_limit_bytes=60 * 1024 * 1024
         ),
     )(tokens, cotangent, routes.T, gates.T, w_gate, w_up, w_down)
+    return both[0], both[1]
 
 
 def solution(mesh):

time: 99.7 us -> 101 us (1.013)
  Pallas kernels: 95.3 us -> 98 us
  local copies, waits for them, and re-layouts: 2.65 us -> 1.35 us
    pallas_call x1, Pallas kernels: 95.3 us -> 98 us  [shards(): pl.pallas_call(functools.partial(kernel, cap, nz), out_shape=out, in_spec...]
    unnamed x2 -> x0, local copies, waits for them, and re-layouts: 2.65 us -> none
    squeeze x0 -> x1, local copies, waits for them, and re-layouts: none -> 1.35 us  [shards(): return (both[0], both[1])]
where the time goes in v4:
time: 101 us; the launch traced here: 100 us
  Pallas kernels  98 us (97%)
  local copies, waits for them, and re-layouts  1.35 us (1%)
    pallas_call x1, Pallas kernels, shards(): pl.pallas_call(functools.partial(kernel, cap, nz), out_shape=out, in_spec...  98 us

profile of v4, /device:TPU:1, one launch (start us, length us, event | category | flops | bytes accessed | tf_op | source)
XLA Modules:
  0.0 100.0 jit_solution(3779484522056813621)
XLA Ops:
  0.6 98.0 %moe_layer.1 = bf16[2,64,128]{2,1,0:T(8,128)(2,1)} custom-call(bf16[64,128]{1,0:T(8,128)(2,1)} %tok_hbm.1, bf16[64,128]{1,0:T(8,128)(2,1)} %cot_hbm.1, s32[2,64]{1,0:T(2,128)} %bitcast.6, f32[2,64]{1,0:T(2,128)} %bitcast.7, bf16[1,4096,384]{2,1,0:T(8,128)(2,1)} %wg_hbm.1, bf16[1,4096,384]{2,1,0:T(8,128)(2,1)} %wu_hbm.1, bf16[1,384,4096]{2,1,0:T(8,128)(2,1)} %wd_hbm.1), custom_call_target="tpu_custom_call" | custom-call | flops 7247757312 | bytes 9437184 | tf_op jit(solution)/shard_map/moe_layer/pallas_call | solution.py:439
  98.7 1.3 %slice_bitcast_fusion = (bf16[64,128]{1,0:T(8,128)(2,1)}, bf16[64,128]{1,0:T(8,128)(2,1)}) fusion(bf16[2,64,128]{2,1,0:T(8,128)(2,1)} %moe_layer.1), kind=kLoop, calls=%fused_computation | loop fusion | bytes 65536 | tf_op jit(solution)/shard_map/squeeze | solution.py:495

commit v5 on v3

--- a/solution.py
+++ b/solution.py
@@ -11,6 +11,7 @@
 F32 = jnp.float32
 BF16 = jnp.bfloat16
 NT = (((1,), (1,)), ((), ()))
+OUTER = (4,)
 
 
 def kernel(
@@ -23,8 +24,7 @@
     wg_hbm,
     wu_hbm,
     wd_hbm,
-    mixed_ref,
-    grad_ref,
+    out_ref,
     wg,
     wu,
     wd,
@@ -91,12 +91,12 @@
         return pl.ds(pl.multiple_of(lax.rem(z + offset + nz, nz) * cols, cols), cols)
 
     def places(j):
-        return {0: (0, 1), 1: (0, 2), last + 1: (1, 3)}.get(j, (0, 4))
+        return {0: (0, 1), 1: (0, 2), last + 1: (1, 3)}.get(j, (0, 6 if j - 1 in OUTER else 4))
 
     def offset(j, s):
         if j == last + 1 and s == 1:
             return nz // 2
-        return (1 if s % 2 else -1) * (hop * j if s < 2 else hop * j - 4)
+        return (1 if s % 2 else -1) * (hop * j - (0, 4, 2)[s // 2])
 
     def joined(blocks, axis):
         return blocks[0] if len(blocks) == 1 else jnp.concatenate(blocks, axis=axis)
@@ -140,6 +140,10 @@
         part = pl.ds(d * toks, toks)
         return remote(raw.at[last, d, part], raw.at[last + 1, 1, part], raw_s.at[i], raw_r.at[i], at_z(1 - 2 * d))
 
+    def outer_copy(j, d):
+        i = 4 * last + 2 + 2 * j + d
+        return remote(raw.at[j, d], raw.at[j + 1, 4 + d], raw_s.at[i], raw_r.at[i], at_z(1 - 2 * d))
+
     def exchange(j, out, into, send, recv):
         a, n = places(j)
         for i in range(1, ne):
@@ -171,7 +175,7 @@
 
     def pass_on(j):
         exchanged(j, slots, y_s, y_r).wait_recv()
-        if j < last:
+        if j < last and j not in OUTER:
             for d in range(2):
                 odd_copy(j, d).start()
 
@@ -180,7 +184,7 @@
         if j is not None:
             a, n = places(j)
             parts += [(slots[j, s], offset(j, s)) for s in range(a, a + n)]
-        if o >= 0:
+        if o >= 0 and o not in OUTER:
             for d in range(2):
                 odd_copy(o, d).wait_recv()
                 parts.append((odd[o, d], (2 * d - 1) * (hop * o + 1)))
@@ -253,9 +257,13 @@
             else:
                 far_copy(d).start()
             fill_copy(j, d).start()
+            if j in OUTER:
+                outer_copy(j, d).start()
         if j > 1:
             for d in range(2):
                 fill_copy(j - 1, d).wait_recv()
+                if j - 1 in OUTER:
+                    outer_copy(j - 1, d).wait_recv()
         dispatch(j)
         pass_on(j - 1)
         if j == 1:
@@ -306,6 +314,8 @@
         return remote(odd_out.at[j, d], odd_in.at[j, d], po_s.at[i], po_r.at[i], at_z(2 * d - 1))
 
     def send_odd(j):
+        if j in OUTER:
+            return
         for d, block in enumerate(partial([-hop * j - 1, hop * j + 1])):
             odd_out[j, d] = block.astype(BF16)
             po_copy(j, d).start()
@@ -313,7 +323,7 @@
     def send_group(j):
         a, n = places(j)
         total = partial([offset(j, s) for s in range(a, a + n)])
-        if j < last:
+        if j < last and j not in OUTER:
             for d in range(2):
                 po_copy(j, d).wait_recv()
                 to = 0 if j == 0 else d
@@ -326,6 +336,10 @@
         i = 2 * (j - 1) + d
         return remote(fill_out.at[j, d], fill_in.at[j, d], f_s.at[i], f_r.at[i], at_z(1 - 2 * d))
 
+    def back_outer(j, d):
+        i = 2 * last + 2 + 2 * j + d
+        return remote(fill_out.at[j, 2 + d], fill_in.at[j, 2 + d], f_s.at[i], f_r.at[i], at_z(2 * d - 1))
+
     def back_far(d):
         i = 2 * last + d
         part = pl.ds(d * toks, toks)
@@ -340,7 +354,7 @@
         exchanged(j, home, b_s, b_r).wait_recv()
         block = joined([home[j, s].reshape(rows, cols) for s in range(a, a + n)], 1)
         picked = jnp.dot(pick_ref[...], block, preferred_element_type=F32)
-        sums = [None] * 4
+        sums = [None] * 6
         for s in range(n):
             one = picked[:, s * cols : (s + 1) * cols]
             mixed = gate_cols[0] * one[:toks] + gate_cols[1] * one[toks : 2 * toks]
@@ -349,6 +363,9 @@
             for d in range(2):
                 fill_out[j - 1, d] = sums[2 + d].astype(BF16)
                 back_fill(j - 1, d).start()
+                if j - 1 in OUTER and j <= last:
+                    fill_out[j - 1, 2 + d] = sums[4 + d].astype(BF16)
+                    back_outer(j - 1, d).start()
         if j == last + 1:
             fill_out[0, 0] = sums[1].astype(BF16)
             for d in range(2):
@@ -360,6 +377,9 @@
         for d in range(2):
             back_fill(j, d).wait_recv()
             total = sums[d] + fill_in[j, d].astype(F32)
+            if j in OUTER:
+                back_outer(j, d).wait_recv()
+                total = total + fill_in[j, 2 + d].astype(F32)
             if j == last:
                 back_far(d).wait_recv()
                 half = far_in[d * toks : (d + 1) * toks, :].astype(F32)
@@ -395,16 +415,20 @@
         far_copy(d).wait_send()
         back_far(d).wait_send()
         for j in range(last):
-            odd_copy(j, d).wait_send()
-            po_copy(j, d).wait_send()
+            if j in OUTER:
+                outer_copy(j, d).wait_send()
+                back_outer(j, d).wait_send()
+            else:
+                odd_copy(j, d).wait_send()
+                po_copy(j, d).wait_send()
     for j in range(last + 2):
         exchanged(j, slots, y_s, y_r).wait_send()
         exchanged(j, home, b_s, b_r).wait_send()
     for d in range(2):
         chain_copy(1, d).wait_recv()
         sums = sums + chain_in[0, d].astype(F32)
-    mixed_ref[...] = sums[:toks].astype(BF16)
-    grad_ref[...] = sums[toks:].astype(BF16)
+    out_ref[0] = sums[:toks].astype(BF16)
+    out_ref[1] = sums[toks:].astype(BF16)
 
 
 def shards(tokens, cotangent, routes, gates, w_gate, w_up, w_down):
@@ -419,21 +443,21 @@
     vmem = pl.BlockSpec(memory_space=pltpu.VMEM)
     hbm = pl.BlockSpec(memory_space=pl.ANY)
     dma = pltpu.SemaphoreType.DMA
-    out = jax.ShapeDtypeStruct((toks, cols), BF16)
-    staged = pltpu.VMEM((groups, ne, 4, pair, cols), BF16)
-    landed = pltpu.VMEM((groups, 4, ne, pair, cols), BF16)
+    out = jax.ShapeDtypeStruct((2, toks, cols), BF16)
+    staged = pltpu.VMEM((groups, ne, 6, pair, cols), BF16)
+    landed = pltpu.VMEM((groups, 6, ne, pair, cols), BF16)
     flat = pltpu.VMEM((last, 2, rows, cols), BF16)
-    tokens_of = pltpu.VMEM((last + 1, 2, 2 * toks, cols), BF16)
-    return pl.pallas_call(
+    tokens_of = pltpu.VMEM((last + 1, 4, 2 * toks, cols), BF16)
+    both = pl.pallas_call(
         functools.partial(kernel, cap, nz),
-        out_shape=(out, out),
+        out_shape=out,
         in_specs=[hbm] * 7,
-        out_specs=(vmem, vmem),
+        out_specs=vmem,
         scratch_shapes=[
             pltpu.VMEM((width, hidden), BF16),
             pltpu.VMEM((width, hidden), BF16),
             pltpu.VMEM((hidden, width), BF16),
-            pltpu.VMEM((groups, 4, 2 * toks, cols), BF16),
+            pltpu.VMEM((groups, 6, 2 * toks, cols), BF16),
             staged,
             landed,
             pltpu.VMEM((last, 2, ne, pair, cols), BF16),
@@ -457,8 +481,8 @@
             tokens_of,
             tokens_of,
             dma((7,)),
-            dma((4 * last + 2,)),
-            dma((4 * last + 2,)),
+            dma((6 * last + 2,)),
+            dma((6 * last + 2,)),
             dma((groups,)),
             dma((groups,)),
             dma((2 * last,)),
@@ -467,8 +491,8 @@
             dma((2 * last,)),
             dma((groups,)),
             dma((groups,)),
-            dma((2 * last + 2,)),
-            dma((2 * last + 2,)),
+            dma((4 * last + 2,)),
+            dma((4 * last + 2,)),
             dma((2 * last,)),
             dma((2 * last,)),
         ],
@@ -480,6 +504,7 @@
             collective_id=0, has_side_effects=True, vmem_limit_bytes=60 * 1024 * 1024
         ),
     )(tokens, cotangent, routes.T, gates.T, w_gate, w_up, w_down)
+    return both[0], both[1]
 
 
 def solution(mesh):

time: 99.7 us -> 104 us (1.043)
  the two profiles are of different devices: /device:TPU:1 before, /device:TPU:37 now
where the time goes in v5:
time: 104 us; the launch traced here: 103 us
  Pallas kernels  101 us (97%)
  local copies, waits for them, and re-layouts  1.35 us (1%)
    pallas_call x1, Pallas kernels, shards(): pl.pallas_call(functools.partial(kernel, cap, nz), out_shape=out, in_spec...  101 us

profile of v5, /device:TPU:37, one launch (start us, length us, event | category | flops | bytes accessed | tf_op | source)
XLA Modules:
  0.0 103.4 jit_solution(11610630770792406851)
XLA Ops:
  0.6 101.4 %moe_layer.1 = bf16[2,64,128]{2,1,0:T(8,128)(2,1)} custom-call(bf16[64,128]{1,0:T(8,128)(2,1)} %tok_hbm.1, bf16[64,128]{1,0:T(8,128)(2,1)} %cot_hbm.1, s32[2,64]{1,0:T(2,128)} %bitcast.6, f32[2,64]{1,0:T(2,128)} %bitcast.7, bf16[1,4096,384]{2,1,0:T(8,128)(2,1)} %wg_hbm.1, bf16[1,4096,384]{2,1,0:T(8,128)(2,1)} %wu_hbm.1, bf16[1,384,4096]{2,1,0:T(8,128)(2,1)} %wd_hbm.1), custom_call_target="tpu_custom_call" | custom-call | flops 7247757312 | bytes 9437184 | tf_op jit(solution)/shard_map/moe_layer/pallas_call | solution.py:451
  102.0 1.3 %slice_bitcast_fusion = (bf16[64,128]{1,0:T(8,128)(2,1)}, bf16[64,128]{1,0:T(8,128)(2,1)}) fusion(bf16[2,64,128]{2,1,0:T(8,128)(2,1)} %moe_layer.1), kind=kLoop, calls=%fused_computation | loop fusion | bytes 65536 | tf_op jit(solution)/shard_map/squeeze | solution.py:507
